TPU v7x, 32 devices: a whole 2x2x4 slice. The times are simulated.
32 devices in a mesh: groups: 2 (over y), ctx: 4 (over x, core), head: 4 (over z).
Axes of the slice: x: 2, y: 2, z: 4, core: 2. Of those that a mesh axis runs over, the one named last changes fastest.
Arguments:
- queries: bfloat16 [12288, 512], P(('groups', 'ctx', 'head')), parts along dimension 0, may hold values from -8 to 8
- keys: bfloat16 [12288, 512], P(('groups', 'ctx', 'head')), parts along dimension 0, may hold values from -8 to 8
- values: bfloat16 [12288, 512], P(('groups', 'ctx', 'head')), parts along dimension 0, may hold values from -6 to 6
- tile_lists: int32 [96, 16], P(('groups', 'ctx')), parts along dimension 0, may hold values from -8 to 54, as said below
- live_counts: int32 [96], P(('groups', 'ctx')), parts along dimension 0, may hold values from 8 to 16
Outputs:
- attended: bfloat16 [12288, 512], P(('groups', 'ctx', 'head')), parts along dimension 0
There are 2 independent parts, one for each index of `groups`. A program takes and returns all parts, laid end to end along the dimension named above; each array names one. Nothing has to cross between parts.
Inputs may be any that keep to these rules, and one draw needn't show every extreme that they name: `tile_lists`: row t holds t + o for each offset o from -8 to 7 exactly once, the first entry being t itself; entries outside 0 to 47 occur only near the ends of the video.
All inputs are finite; a program needn't handle non-finite values.
Results may differ from a plain program's by a relative error of at most 0.0047.
Values may be sent and summed in bfloat16 or wider, within the bound.
A program may use at most 64 MiB of HBM per device.

v0:
```python
import jax
import jax.numpy as jnp
from jax import lax
from jax.sharding import PartitionSpec as P

HDIM = 128
TILE = 128
EDGE = 8
CTX_TILES = 12
LIST = 16


def with_halo(block, sides, width):
    for axis, dim in sides:
        count = lax.axis_size(axis)
        forward = [(i, i + 1) for i in range(count - 1)]
        backward = [(target, source) for source, target in forward]
        low = lax.ppermute(
            lax.slice_in_dim(block, block.shape[dim] - width, None, axis=dim), axis, forward
        )
        high = lax.ppermute(lax.slice_in_dim(block, 0, width, axis=dim), axis, backward)
        block = jnp.concatenate([low, block, high], axis=dim)
    return block


def block_tiles():
    for candidate in (4, 2, 1):
        return candidate
    return 1


def edge_tiles(kv_pair):
    return with_halo(kv_pair, (("ctx", 1),), EDGE * TILE)


def attend(q_rows, row_lists, row_counts, kv_tiles, query_first, kv_first, total_tiles):
    tile_count = row_lists.shape[0]
    per_block = block_tiles()
    block_count = tile_count // per_block
    window_span = per_block + 2 * EDGE - 1
    score_scale = HDIM ** (-0.5)
    q_blocks = q_rows.reshape(block_count, per_block, TILE, HDIM)
    block_list_entries = row_lists.reshape(block_count, per_block, LIST)
    count_blocks = row_counts.reshape(block_count, per_block)
    block_numbers = jnp.arange(block_count, dtype=jnp.int32)
    positions = jnp.arange(LIST)
    window_steps = jnp.arange(window_span, dtype=jnp.int32)

    def one_block(inputs):
        query_portion, list_part, count_part, block_number = inputs
        block_first = query_first + block_number * per_block
        window_first = block_first - EDGE
        window = lax.dynamic_slice_in_dim(kv_tiles, window_first - kv_first, window_span, 1)
        key_window_tiles = window[0].reshape(window_span * TILE, HDIM)
        value_window_tiles = window[1].reshape(window_span * TILE, HDIM)
        window_ids = window_first + window_steps
        in_range = (window_ids >= 0) & (window_ids < total_tiles)
        live = positions[None, :] < count_part[:, None]
        matched = (list_part[:, :, None] == window_ids[None, None, :]) & live[:, :, None]
        usable = jnp.any(matched, axis=1) & in_range[None, :]
        visible = jnp.repeat(usable, TILE, axis=1)[:, None, :]
        scores = (
            jnp.einsum(
                "tfy,vy->tfv", query_portion, key_window_tiles, preferred_element_type=jnp.float32
            )
            * score_scale
        )
        scores = jnp.where(visible, scores, -1e30)
        highest = jnp.max(scores, axis=-1, keepdims=True)
        weights = jnp.where(visible, jnp.exp(scores - highest), 0.0)
        softmax_divisor = jnp.sum(weights, axis=-1, keepdims=True)
        attention_probs = weights.astype(jnp.bfloat16)
        mixed = jnp.einsum(
            "jzn,nw->jzw", attention_probs, value_window_tiles, preferred_element_type=jnp.float32
        )
        return (mixed / softmax_divisor).astype(jnp.bfloat16)

    results = lax.map(one_block, (q_blocks, block_list_entries, count_blocks, block_numbers))
    return results.reshape(tile_count * TILE, HDIM)


def on_device(queries, keys, values, tile_lists, live_counts):
    ctx_count = lax.axis_size("ctx")
    total_tiles = CTX_TILES * ctx_count
    first_tile = lax.axis_index("ctx") * CTX_TILES
    kv_pair = lax.all_to_all(
        jnp.stack([keys, values]), "head", split_axis=2, concat_axis=1, tiled=True
    )
    padded = edge_tiles(kv_pair)
    local_q = lax.all_to_all(queries, "head", split_axis=1, concat_axis=0, tiled=True)
    padded_count = CTX_TILES + 2 * EDGE
    padded_tiles = padded.reshape(2, padded_count, TILE, HDIM)
    head_out = attend(
        local_q, tile_lists, live_counts, padded_tiles, first_tile, first_tile - EDGE, total_tiles
    )
    return lax.all_to_all(head_out, "head", split_axis=0, concat_axis=1, tiled=True)


def solution(mesh):
    return jax.shard_map(
        on_device,
        mesh=mesh,
        in_specs=(
            P(("groups", "ctx", "head"), None),
            P(("groups", "ctx", "head"), None),
            P(("groups", "ctx", "head"), None),
            P(("groups", "ctx"), None),
            P(("groups", "ctx")),
        ),
        out_specs=P(("groups", "ctx", "head"), None),
        check_vma=False,
    )
```

profile of v0, /device:TPU:0, one launch (start us, length us, event | category | flops | bytes accessed | tf_op | source)
XLA Modules:
  0.0 94.4 jit_solution(12368793994641363082)
XLA Ops:
  0.0 1.2 %pad_maximum_fusion.1 = bf16[2,384,512]{2,1,0:T(8,128)(2,1)S(1)} fusion(bf16[1,384,512]{2,1,0:T(8,128)(2,1)} %bitcast.91, bf16[1,384,512]{2,1,0:T(8,128)(2,1)} %bitcast.92), kind=kLoop, calls=%fused_computation.40 | loop fusion | flops 393216 | bytes 1572864 | tf_op jit(solution)/shard_map/stack | solution.py:87
  1.2 1.1 %copy.26 = bf16[2,384,512]{1,0,2:T(2,128)(2,1)S(1)} copy(bf16[2,384,512]{2,1,0:T(8,128)(2,1)S(1)} %pad_maximum_fusion.1) | data formatting | bytes 1572864 | tf_op jit(solution)/shard_map/stack | solution.py:87
  2.4 26.2 %all_to_all.53 = bf16[2,384,512]{1,0,2:T(2,128)(2,1)S(1)} all-to-all(bf16[2,384,512]{1,0,2:T(2,128)(2,1)S(1)} %copy.26), channel_id=1, replica_groups=mesh['groups'=2,'ctx'=4,'head'=4] {'head'}, dimensions={2} | all-to-all | bytes 1572864 | tf_op jit(solution)/shard_map/all_to_all | solution.py:86
  28.7 0.4 copy.28
  29.2 1.3 %collective-permute-start = (bf16[2,1024,128]{2,1,0:T(8,128)(2,1)S(1)}, bf16[2,1024,128]{2,1,0:T(8,128)(2,1)S(1)}, u32[]{:S(2)}, u32[]{:S(2)}) collective-permute-start(bf16[2,1024,128]{2,1,0:T(8,128)(2,1)S(1)} %get-tuple-element.184), channel_id=1, source_target_pairs={{0,4},{4,8},{8,12},{1,5},{5,9},{9,13},{2,6},{6,10},{10,14},{3,7},{... | collective-permute-start | bytes 1572872 | tf_op jit(solution)/shard_map/ppermute | solution.py:18
  30.5 1.3 %collective-permute-start.1 = (bf16[2,1024,128]{2,1,0:T(8,128)(2,1)S(1)}, bf16[2,1024,128]{2,1,0:T(8,128)(2,1)}, u32[]{:S(2)}, u32[]{:S(2)}) collective-permute-start(bf16[2,1024,128]{2,1,0:T(8,128)(2,1)S(1)} %get-tuple-element.185), channel_id=1, source_target_pairs={{4,0},{8,4},{12,8},{5,1},{9,5},{13,9},{6,2},{10,6},{14,10},{7,3},{... | collective-permute-start | bytes 1572872 | tf_op jit(solution)/shard_map/ppermute | solution.py:21
  31.8 0.8 copy_bitcast_fusion.1
  32.7 4.1 %all-to-all-start = ((bf16[384,4,128]{2,0,1:T(8,128)(2,1)}), bf16[384,4,128]{2,0,1:T(8,128)(2,1)}, u32[]{:S(2)}, u32[]{:S(2)}) async-start(bf16[384,4,128]{2,0,1:T(8,128)(2,1)} %copy_bitcast_fusion.1), calls=%async_computation | async-start | bytes 786432 | tf_op jit(solution)/shard_map/all_to_all | solution.py:90
  36.9 1.2 %pad_maximum_fusion = bf16[2,3584,128]{2,1,0:T(8,128)(2,1)S(1)} fusion(bf16[2,1024,128]{2,1,0:T(8,128)(2,1)} %collective-permute-done.1, bf16[2,1536,128]{2,1,0:T(8,128)(2,1)S(1)} %bitcast.87, bf16[2,1024,128]{2,1,0:T(8,128)(2,1)S(1)} %collective-permute-done), kind=kLoop, calls=%fused_computation.39 | loop fusion | flops 5505024 | bytes 3670016 | tf_op jit(solution)/shard_map/concatenate | solution.py:22
  38.1 9.7 %all-to-all-done = bf16[384,4,128]{2,0,1:T(8,128)(2,1)} async-done(((bf16[384,4,128]{2,0,1:T(8,128)(2,1)}), bf16[384,4,128]{2,0,1:T(8,128)(2,1)}, u32[]{:S(2)}, u32[]{:S(2)}) %all-to-all-start) | async-done | bytes 393248 | tf_op jit(solution)/shard_map/all_to_all | solution.py:90
  47.8 28.5 %while.13 = (s32[]{:T(128)}, bf16[3,4,128,128]{3,2,1,0:T(8,128)(2,1)}, s32[3,4,16]{2,1,0:T(4,128)S(1)}, s32[3]{0:T(128)S(1)}, s32[]{:T(128)}, /*index=5*/s32[3,4...) while((s32[]{:T(128)}, ...), condition=%wide.region_4.5_spmd.clone, body=%wide.region_0.4_spmd.clone.sunk | while | flops 968893440 | bytes 4826797 | solution.py:78
  47.8 0.6 dynamic_slice.67
  49.1 0.1 constant_dynamic-slice_fusion.4
  49.6 3.1 %fusion.73 = f32[4,128]{1,0:T(4,128)S(1)} fusion(bf16[2432,128,1]{1,0,2:T(8,128)(2,1)S(1)} %bitcast.83, pred[4,2432]{1,0:T(4,128)(4,1)S(1)} %bitcast.93, bf16[3,4,128,128]{3,2,1,0:T(8,128)(2,1)} %get-tuple-element.281, s32[]{:T(128)} %get-tuple-element.260), kind=kOutput, calls=%fused_computation.42.clone.1 | convolution fusion | flops 324995456 | bytes 775680 | tf_op jit(solution)/shard_map/while/body/eval_jaxpr/sub | solution.py:70
  52.7 4.6 %fusion.74 = bf16[3,4,128,128]{3,2,1,0:T(8,128)(2,1)} fusion(bf16[3,4,128,128]{3,2,1,0:T(8,128)(2,1)} %get-tuple-element.261, s32[]{:T(128)} %get-tuple-element.260, bf16[2432,128,1]{1,0,2:T(8,128)(2,1)S(1)} %bitcast.85, f32[4,128]{1,0:T(4,128)S(1)} %fusion.73, pred[4,2432]{1,0:T(4,128)(4,1)S(1)} %bitcast.94, ...), kind=kOutput, calls=%fused_computation.12.clone.1 | convolution fusion | flops 643894144 | bytes 1529856 | tf_op jit(solution)/shard_map/while/body/eval_jaxpr/jzn,nw->jzw/dot_general | solution.py:73
  57.3 0.6 dynamic_slice.67
  59.0 3.2 %fusion.73 = f32[4,128]{1,0:T(4,128)S(1)} fusion(bf16[2432,128,1]{1,0,2:T(8,128)(2,1)S(1)} %bitcast.83, pred[4,2432]{1,0:T(4,128)(4,1)S(1)} %bitcast.93, bf16[3,4,128,128]{3,2,1,0:T(8,128)(2,1)} %get-tuple-element.281, s32[]{:T(128)} %get-tuple-element.260), kind=kOutput, calls=%fused_computation.42.clone.1 | convolution fusion | flops 324995456 | bytes 775680 | tf_op jit(solution)/shard_map/while/body/eval_jaxpr/sub | solution.py:70
  62.2 4.6 %fusion.74 = bf16[3,4,128,128]{3,2,1,0:T(8,128)(2,1)} fusion(bf16[3,4,128,128]{3,2,1,0:T(8,128)(2,1)} %get-tuple-element.261, s32[]{:T(128)} %get-tuple-element.260, bf16[2432,128,1]{1,0,2:T(8,128)(2,1)S(1)} %bitcast.85, f32[4,128]{1,0:T(4,128)S(1)} %fusion.73, pred[4,2432]{1,0:T(4,128)(4,1)S(1)} %bitcast.94, ...), kind=kOutput, calls=%fused_computation.12.clone.1 | convolution fusion | flops 643894144 | bytes 1529856 | tf_op jit(solution)/shard_map/while/body/eval_jaxpr/jzn,nw->jzw/dot_general | solution.py:73
  66.8 0.6 dynamic_slice.67
  68.5 3.2 %fusion.73 = f32[4,128]{1,0:T(4,128)S(1)} fusion(bf16[2432,128,1]{1,0,2:T(8,128)(2,1)S(1)} %bitcast.83, pred[4,2432]{1,0:T(4,128)(4,1)S(1)} %bitcast.93, bf16[3,4,128,128]{3,2,1,0:T(8,128)(2,1)} %get-tuple-element.281, s32[]{:T(128)} %get-tuple-element.260), kind=kOutput, calls=%fused_computation.42.clone.1 | convolution fusion | flops 324995456 | bytes 775680 | tf_op jit(solution)/shard_map/while/body/eval_jaxpr/sub | solution.py:70
  71.7 4.6 %fusion.74 = bf16[3,4,128,128]{3,2,1,0:T(8,128)(2,1)} fusion(bf16[3,4,128,128]{3,2,1,0:T(8,128)(2,1)} %get-tuple-element.261, s32[]{:T(128)} %get-tuple-element.260, bf16[2432,128,1]{1,0,2:T(8,128)(2,1)S(1)} %bitcast.85, f32[4,128]{1,0:T(4,128)S(1)} %fusion.73, pred[4,2432]{1,0:T(4,128)(4,1)S(1)} %bitcast.94, ...), kind=kOutput, calls=%fused_computation.12.clone.1 | convolution fusion | flops 643894144 | bytes 1529856 | tf_op jit(solution)/shard_map/while/body/eval_jaxpr/jzn,nw->jzw/dot_general | solution.py:73
  76.3 16.9 %all_to_all.54 = bf16[4,384,128]{2,1,0:T(8,128)(2,1)S(1)} all-to-all(bf16[4,384,128]{2,1,0:T(8,128)(2,1)} %bitcast.90), channel_id=1, replica_groups=mesh['groups'=2,'ctx'=4,'head'=4] {'head'}, dimensions={0} | all-to-all | bytes 786432 | tf_op jit(solution)/shard_map/all_to_all | solution.py:96
  93.2 0.2 copy.29
  93.5 0.9 copy.30
  (43 shorter events, 1.5 us)
Async XLA Ops:
  0.0 31.8 %copy-start = (bf16[384,512]{1,0:T(8,128)(2,1)S(1)}, bf16[384,512]{1,0:T(8,128)(2,1)}, u32[]{:S(2)}) copy-start(bf16[384,512]{1,0:T(8,128)(2,1)} %param.7) | copy-start | bytes 1179652
  29.1 7.7 %copy-start.1 = (s32[12,16]{1,0:T(8,128)S(1)}, s32[12,16]{1,0:T(8,128)}, u32[]{:S(2)}) copy-start(s32[12,16]{1,0:T(8,128)} %param.10) | copy-start | bytes 2308
  29.1 7.7 %copy-start.2 = (s32[12]{0:T(128)S(1)}, s32[12]{0:T(128)}, u32[]{:S(2)}) copy-start(s32[12]{0:T(128)} %param.11) | copy-start | bytes 148
  29.2 7.7 %collective-permute-start = (bf16[2,1024,128]{2,1,0:T(8,128)(2,1)S(1)}, bf16[2,1024,128]{2,1,0:T(8,128)(2,1)S(1)}, u32[]{:S(2)}, u32[]{:S(2)}) collective-permute-start(bf16[2,1024,128]{2,1,0:T(8,128)(2,1)S(1)} %get-tuple-element.184), channel_id=1, source_target_pairs={{0,4},{4,8},{8,12},{1,5},{5,9},{9,13},{2,6},{6,10},{10,14},{3,7},{... | collective-permute-start | bytes 1572872 | tf_op jit(solution)/shard_map/ppermute | solution.py:18
  30.5 6.4 %collective-permute-start.1 = (bf16[2,1024,128]{2,1,0:T(8,128)(2,1)S(1)}, bf16[2,1024,128]{2,1,0:T(8,128)(2,1)}, u32[]{:S(2)}, u32[]{:S(2)}) collective-permute-start(bf16[2,1024,128]{2,1,0:T(8,128)(2,1)S(1)} %get-tuple-element.185), channel_id=1, source_target_pairs={{4,0},{8,4},{12,8},{5,1},{9,5},{13,9},{6,2},{10,6},{14,10},{7,3},{... | collective-permute-start | bytes 1572872 | tf_op jit(solution)/shard_map/ppermute | solution.py:21
  32.7 15.2 %all-to-all-start = ((bf16[384,4,128]{2,0,1:T(8,128)(2,1)}), bf16[384,4,128]{2,0,1:T(8,128)(2,1)}, u32[]{:S(2)}, u32[]{:S(2)}) async-start(bf16[384,4,128]{2,0,1:T(8,128)(2,1)} %copy_bitcast_fusion.1), calls=%async_computation | async-start | bytes 786432 | tf_op jit(solution)/shard_map/all_to_all | solution.py:90
where the time goes:
time: 94.9 us; the launch traced here: 94.4 us
  blocking collectives  43.2 us (46%)
  matrix products  23.3 us (25%)
  waiting for transfers between devices  9.74 us (10%)
  starting transfers between devices  6.73 us (7%)
  local copies, waits for them, and re-layouts  6.34 us (7%)
  other arithmetic  2.97 us (3%)
  loops' own time  2.05 us (2%)
    all_to_all x1, blocking collectives, on_device(): lax.all_to_all(jnp.stack([keys, values]), 'head', split_axis=2, concat_ax...  26.2 us
    all_to_all x1, blocking collectives, on_device(): lax.all_to_all(head_out, 'head', split_axis=0, concat_axis=1, tiled=True)  16.9 us
    dot_general x3, matrix products, one_block(): jnp.einsum('jzn,nw->jzw', attention_probs, value_window_tiles, preferred_...  13.8 us
    all_to_all x1, waiting for transfers between devices, on_device(): lax.all_to_all(queries, 'head', split_axis=1, concat_axis=0, tiled=True)  9.74 us
    sub x3, matrix products, one_block(): weights = jnp.where(visible, jnp.exp(scores - highest), 0.0)  9.46 us
    all_to_all x1, starting transfers between devices, on_device(): lax.all_to_all(queries, 'head', split_axis=1, concat_axis=0, tiled=True)  4.11 us
    another operation x1, loops' own time, attend(): lax.map(one_block, (q_blocks, block_list_entries, count_blocks, block_num...  2.05 us
  transfers between devices with their start and end apart: 3, of which 1 were waited for; matrix products, arithmetic and copies ran while one was open for 2% of the time, Pallas kernels for 0%

commit v1 on v0

--- a/solution.py
+++ b/solution.py
@@ -8,6 +8,17 @@
 EDGE = 8
 CTX_TILES = 12
 LIST = 16
+
+
+def cut_along(array, dim, size):
+    before, after = (array.shape[:dim], array.shape[dim + 1 :])
+    return jnp.moveaxis(array.reshape(*before, size, -1, *after), dim, 0)
+
+
+def in_order(pieces, dim):
+    pieces = jnp.moveaxis(pieces, 0, dim)
+    lengths = pieces.shape
+    return pieces.reshape(*lengths[:dim], lengths[dim] * lengths[dim + 1], *lengths[dim + 2 :])
 
 
 def with_halo(block, sides, width):
@@ -87,7 +98,14 @@
         jnp.stack([keys, values]), "head", split_axis=2, concat_axis=1, tiled=True
     )
     padded = edge_tiles(kv_pair)
-    local_q = lax.all_to_all(queries, "head", split_axis=1, concat_axis=0, tiled=True)
+    size, index = (lax.axis_size("head"), lax.axis_index("head"))
+    pieces = cut_along(queries, 1, size)
+    outs = [pieces[index]]
+    for step in range(1, size):
+        sent = pieces[index ^ step]
+        outs.append(lax.ppermute(sent, "head", [(i_2, i_2 ^ step) for i_2 in range(size)]))
+    pieces = jnp.stack(outs)[index ^ jnp.arange(size)]
+    local_q = in_order(pieces, 0)
     padded_count = CTX_TILES + 2 * EDGE
     padded_tiles = padded.reshape(2, padded_count, TILE, HDIM)
     head_out = attend(

time: 94.9 us -> 91.6 us (0.965)
  waiting for transfers between devices: 9.74 us -> 4.3 us
  local copies, waits for them, and re-layouts: 6.34 us -> 8.41 us
  matrix products: 23.3 us -> 21.4 us
    all_to_all x1 -> x0, waiting for transfers between devices: 9.74 us -> none  [on_device(): lax.all_to_all(queries, 'head', split_axis=1, concat_axis=0, tiled=True)]
    ppermute x0 -> x3, starting transfers between devices: none -> 4.58 us  [on_device(): lax.ppermute(sent, 'head', [(i_2, i_2 ^ step) for i_2 in range(size)])]
    ppermute x0 -> x3, waiting for transfers between devices: none -> 4.3 us  [on_device(): lax.ppermute(sent, 'head', [(i_2, i_2 ^ step) for i_2 in range(size)])]
    all_to_all x1 -> x0, starting transfers between devices: 4.11 us -> none  [on_device(): lax.all_to_all(queries, 'head', split_axis=1, concat_axis=0, tiled=True)]
    dot_general x3, matrix products: 13.8 us -> 12 us  [one_block(): jnp.einsum('jzn,nw->jzw', attention_probs, value_window_tiles, preferred_...]
    gather x0 -> x1, local copies, waits for them, and re-layouts: none -> 1.34 us  [on_device(): pieces = jnp.stack(outs)[index ^ jnp.arange(size)]]
  transfers between devices with their start and end apart: 3 -> 5, of which waited for: 1 -> 2; matrix products, arithmetic and copies ran while one was open for 2% -> 4% of each run, Pallas kernels for 0% -> 0%
where the time goes in v1:
time: 91.6 us; the launch traced here: 91.1 us
  blocking collectives  43.4 us (47%)
  matrix products  21.4 us (23%)
  local copies, waits for them, and re-layouts  8.41 us (9%)
  starting transfers between devices  7.2 us (8%)
  waiting for transfers between devices  4.3 us (5%)
  other arithmetic  3.87 us (4%)
  loops' own time  2.35 us (3%)
    all_to_all x1, blocking collectives, on_device(): lax.all_to_all(jnp.stack([keys, values]), 'head', split_axis=2, concat_ax...  26.2 us
    all_to_all x1, blocking collectives, on_device(): lax.all_to_all(head_out, 'head', split_axis=0, concat_axis=1, tiled=True)  17.1 us
    dot_general x3, matrix products, one_block(): jnp.einsum('jzn,nw->jzw', attention_probs, value_window_tiles, preferred_...  12 us
    sub x3, matrix products, one_block(): weights = jnp.where(visible, jnp.exp(scores - highest), 0.0)  9.45 us
    ppermute x3, starting transfers between devices, on_device(): lax.ppermute(sent, 'head', [(i_2, i_2 ^ step) for i_2 in range(size)])  4.58 us
    ppermute x3, waiting for transfers between devices, on_device(): lax.ppermute(sent, 'head', [(i_2, i_2 ^ step) for i_2 in range(size)])  4.3 us
    another operation x1, loops' own time, attend(): lax.map(one_block, (q_blocks, block_list_entries, count_blocks, block_num...  2.35 us
    dynamic_slice x3, local copies, waits for them, and re-layouts, attend(): lax.map(one_block, (q_blocks, block_list_entries, count_blocks, block_num...  2 us
  transfers between devices with their start and end apart: 5, of which 2 were waited for; matrix products, arithmetic and copies ran while one was open for 4% of the time, Pallas kernels for 0%

profile of v1, /device:TPU:0, one launch (start us, length us, event | category | flops | bytes accessed | tf_op | source)
XLA Modules:
  0.0 91.1 jit_solution(3516511065728472409)
XLA Ops:
  0.0 1.2 %pad_maximum_fusion.1 = bf16[2,384,512]{2,1,0:T(8,128)(2,1)S(1)} fusion(bf16[1,384,512]{2,1,0:T(8,128)(2,1)} %bitcast.96, bf16[1,384,512]{2,1,0:T(8,128)(2,1)} %bitcast.97), kind=kLoop, calls=%fused_computation.41 | loop fusion | flops 393216 | bytes 1572864 | tf_op jit(solution)/shard_map/stack | solution.py:98
  1.2 1.1 %copy.47 = bf16[2,384,512]{1,0,2:T(2,128)(2,1)S(1)} copy(bf16[2,384,512]{2,1,0:T(8,128)(2,1)S(1)} %pad_maximum_fusion.1) | data formatting | bytes 1572864 | tf_op jit(solution)/shard_map/stack | solution.py:98
  2.3 26.2 %all_to_all.37 = bf16[2,384,512]{1,0,2:T(2,128)(2,1)S(1)} all-to-all(bf16[2,384,512]{1,0,2:T(2,128)(2,1)S(1)} %copy.47), channel_id=1, replica_groups=mesh['groups'=2,'ctx'=4,'head'=4] {'head'}, dimensions={2} | all-to-all | bytes 1572864 | tf_op jit(solution)/shard_map/all_to_all | solution.py:97
  29.1 1.3 %collective-permute-start.3 = (bf16[2,1024,128]{2,1,0:T(8,128)(2,1)S(1)}, bf16[2,1024,128]{2,1,0:T(8,128)(2,1)S(1)}, u32[]{:S(2)}, u32[]{:S(2)}) collective-permute-start(bf16[2,1024,128]{2,1,0:T(8,128)(2,1)S(1)} %get-tuple-element.184), channel_id=1, source_target_pairs={{0,4},{4,8},{8,12},{1,5},{5,9},{9,13},{2,6},{6,10},{10,14},{3,7},{... | collective-permute-start | bytes 1572872 | tf_op jit(solution)/shard_map/ppermute | solution.py:29
  30.5 1.3 %collective-permute-start.4 = (bf16[2,1024,128]{2,1,0:T(8,128)(2,1)S(1)}, bf16[2,1024,128]{2,1,0:T(8,128)(2,1)}, u32[]{:S(2)}, u32[]{:S(2)}) collective-permute-start(bf16[2,1024,128]{2,1,0:T(8,128)(2,1)S(1)} %get-tuple-element.185), channel_id=1, source_target_pairs={{4,0},{8,4},{12,8},{5,1},{9,5},{13,9},{6,2},{10,6},{14,10},{7,3},{... | collective-permute-start | bytes 1572872 | tf_op jit(solution)/shard_map/ppermute | solution.py:32
  32.6 1.9 %collective-permute-start.1 = (bf16[384,128]{1,0:T(8,128)(2,1)S(1)}, bf16[384,128]{1,0:T(8,128)(2,1)S(1)}, u32[]{:S(2)}, u32[]{:S(2)}) collective-permute-start(bf16[384,128]{1,0:T(8,128)(2,1)S(1)} %bitcast.104), channel_id=1, source_target_pairs={{0,2},{1,3},{2,0},{3,1},{4,6},{5,7},{6,4},{7,5},{8,10},{9,11},{10,... | collective-permute-start | bytes 294920 | tf_op jit(solution)/shard_map/ppermute | solution.py:106
  34.6 2.4 %collective-permute-start.2 = (bf16[384,128]{1,0:T(8,128)(2,1)S(1)}, bf16[384,128]{1,0:T(8,128)(2,1)}, u32[]{:S(2)}, u32[]{:S(2)}) collective-permute-start(bf16[384,128]{1,0:T(8,128)(2,1)S(1)} %bitcast.105), channel_id=1, source_target_pairs={{0,3},{1,2},{2,1},{3,0},{4,7},{5,6},{6,5},{7,4},{8,11},{9,10},{10,... | collective-permute-start | bytes 294920 | tf_op jit(solution)/shard_map/ppermute | solution.py:106
  37.2 0.7 reshape.94
  38.3 4.0 %collective-permute-done.2 = bf16[384,128]{1,0:T(8,128)(2,1)} collective-permute-done((bf16[384,128]{1,0:T(8,128)(2,1)S(1)}, bf16[384,128]{1,0:T(8,128)(2,1)}, u32[]{:S(2)}, u32[]{:S(2)}) %collective-permute-start.2) | collective-permute-done | bytes 98336 | tf_op jit(solution)/shard_map/ppermute | solution.py:106
  42.3 0.9 %pad_maximum_fusion.2 = bf16[4,384,128]{2,1,0:T(8,128)(2,1)S(1)} fusion(bf16[1,384,128]{2,1,0:T(8,128)(2,1)} %bitcast.7, bf16[1,384,128]{2,1,0:T(8,128)(2,1)S(1)} %bitcast.102, bf16[1,384,128]{2,1,0:T(8,128)(2,1)S(1)} %bitcast.101, bf16[1,384,128]{2,1,0:T(8,128)(2,1)S(1)} %bitcast.95), kind=kLoop, calls=%fused_computation.42 | loop fusion | flops 589824 | bytes 786432 | tf_op jit(solution)/shard_map/stack | solution.py:107
  43.2 1.3 %gather_fusion = bf16[4,384,128]{2,1,0:T(8,128)(2,1)} fusion(bf16[4,384,128]{2,1,0:T(8,128)(2,1)S(1)} %pad_maximum_fusion.2, s32[1024]{0:T(1024)S(1)} %pad_clamp_fusion), kind=kCustom, calls=%fused_computation | custom fusion | bytes 786448 | tf_op jit(solution)/shard_map/gather | solution.py:107
  44.6 1.2 %pad_maximum_fusion = bf16[2,3584,128]{2,1,0:T(8,128)(2,1)S(1)} fusion(bf16[2,1024,128]{2,1,0:T(8,128)(2,1)} %collective-permute-done.4, bf16[2,1536,128]{2,1,0:T(8,128)(2,1)S(1)} %bitcast.90, bf16[2,1024,128]{2,1,0:T(8,128)(2,1)S(1)} %collective-permute-done.3), kind=kLoop, calls=%fused_computation.40 | loop fusion | flops 5505024 | bytes 3670016 | tf_op jit(solution)/shard_map/concatenate | solution.py:33
  45.7 27.1 %while.13 = (s32[]{:T(128)}, bf16[3,4,128,128]{3,2,1,0:T(8,128)(2,1)S(1)}, s32[3,4,16]{2,1,0:T(4,128)S(1)}, s32[3]{0:T(128)S(1)}, s32[]{:T(128)}, /*index=5*/s32...) while((s32[]{:T(128)}, ...), condition=%wide.region_4.5_spmd.clone, body=%wide.region_0.4_spmd.clone.sunk | while | flops 968893440 | bytes 4826797 | solution.py:89
  45.8 0.7 dynamic_slice.74
  47.6 3.1 %fusion.73 = f32[4,128]{1,0:T(4,128)S(1)} fusion(bf16[2432,128,1]{1,0,2:T(8,128)(2,1)S(1)} %bitcast.86, pred[4,2432]{1,0:T(4,128)(4,1)S(1)} %bitcast.99, bf16[3,4,128,128]{3,2,1,0:T(8,128)(2,1)} %get-tuple-element.285, s32[]{:T(128)} %get-tuple-element.264), kind=kOutput, calls=%fused_computation.50.clone.1 | convolution fusion | flops 324995456 | bytes 775680 | tf_op jit(solution)/shard_map/while/body/eval_jaxpr/sub | solution.py:81
  50.8 4.0 %fusion.74 = bf16[3,4,128,128]{3,2,1,0:T(8,128)(2,1)S(1)} fusion(bf16[3,4,128,128]{3,2,1,0:T(8,128)(2,1)S(1)} %get-tuple-element.265, s32[]{:T(128)} %get-tuple-element.264, bf16[2432,128,1]{1,0,2:T(8,128)(2,1)S(1)} %bitcast.88, f32[4,128]{1,0:T(4,128)S(1)} %fusion.73, pred[4,2432]{1,0:T(4,128)(4,1)S(1)} %bitcast.100, ...), kind=kOutput, calls=%fused_computation.13.clone.1 | convolution fusion | flops 643894144 | bytes 1529856 | tf_op jit(solution)/shard_map/while/body/eval_jaxpr/jzn,nw->jzw/dot_general | solution.py:84
  54.8 0.7 dynamic_slice.74
  56.6 3.1 %fusion.73 = f32[4,128]{1,0:T(4,128)S(1)} fusion(bf16[2432,128,1]{1,0,2:T(8,128)(2,1)S(1)} %bitcast.86, pred[4,2432]{1,0:T(4,128)(4,1)S(1)} %bitcast.99, bf16[3,4,128,128]{3,2,1,0:T(8,128)(2,1)} %get-tuple-element.285, s32[]{:T(128)} %get-tuple-element.264), kind=kOutput, calls=%fused_computation.50.clone.1 | convolution fusion | flops 324995456 | bytes 775680 | tf_op jit(solution)/shard_map/while/body/eval_jaxpr/sub | solution.py:81
  59.8 4.0 %fusion.74 = bf16[3,4,128,128]{3,2,1,0:T(8,128)(2,1)S(1)} fusion(bf16[3,4,128,128]{3,2,1,0:T(8,128)(2,1)S(1)} %get-tuple-element.265, s32[]{:T(128)} %get-tuple-element.264, bf16[2432,128,1]{1,0,2:T(8,128)(2,1)S(1)} %bitcast.88, f32[4,128]{1,0:T(4,128)S(1)} %fusion.73, pred[4,2432]{1,0:T(4,128)(4,1)S(1)} %bitcast.100, ...), kind=kOutput, calls=%fused_computation.13.clone.1 | convolution fusion | flops 643894144 | bytes 1529856 | tf_op jit(solution)/shard_map/while/body/eval_jaxpr/jzn,nw->jzw/dot_general | solution.py:84
  63.8 0.7 dynamic_slice.74
  65.7 3.2 %fusion.73 = f32[4,128]{1,0:T(4,128)S(1)} fusion(bf16[2432,128,1]{1,0,2:T(8,128)(2,1)S(1)} %bitcast.86, pred[4,2432]{1,0:T(4,128)(4,1)S(1)} %bitcast.99, bf16[3,4,128,128]{3,2,1,0:T(8,128)(2,1)} %get-tuple-element.285, s32[]{:T(128)} %get-tuple-element.264), kind=kOutput, calls=%fused_computation.50.clone.1 | convolution fusion | flops 324995456 | bytes 775680 | tf_op jit(solution)/shard_map/while/body/eval_jaxpr/sub | solution.py:81
  68.8 4.0 %fusion.74 = bf16[3,4,128,128]{3,2,1,0:T(8,128)(2,1)S(1)} fusion(bf16[3,4,128,128]{3,2,1,0:T(8,128)(2,1)S(1)} %get-tuple-element.265, s32[]{:T(128)} %get-tuple-element.264, bf16[2432,128,1]{1,0,2:T(8,128)(2,1)S(1)} %bitcast.88, f32[4,128]{1,0:T(4,128)S(1)} %fusion.73, pred[4,2432]{1,0:T(4,128)(4,1)S(1)} %bitcast.100, ...), kind=kOutput, calls=%fused_computation.13.clone.1 | convolution fusion | flops 643894144 | bytes 1529856 | tf_op jit(solution)/shard_map/while/body/eval_jaxpr/jzn,nw->jzw/dot_general | solution.py:84
  72.8 17.1 %all_to_all.38 = bf16[4,384,128]{2,1,0:T(8,128)(2,1)S(1)} all-to-all(bf16[4,384,128]{2,1,0:T(8,128)(2,1)S(1)} %bitcast.94), channel_id=1, replica_groups=mesh['groups'=2,'ctx'=4,'head'=4] {'head'}, dimensions={0} | all-to-all | bytes 786432 | tf_op jit(solution)/shard_map/all_to_all | solution.py:114
  90.2 0.9 %copy.51 = bf16[384,512]{1,0:T(8,128)(2,1)} copy(bf16[384,512]{0,1:T(8,128)(2,1)S(1)} %bitcast.93) | data formatting | bytes 786432 | tf_op jit(solution)/shard_map/all_to_all | solution.py:114
  (54 shorter events, 3.4 us)
Async XLA Ops:
  28.7 3.1 %copy-start = (bf16[384,512]{1,0:T(8,128)(2,1)S(1)}, bf16[384,512]{1,0:T(8,128)(2,1)}, u32[]{:S(2)}) copy-start(bf16[384,512]{1,0:T(8,128)(2,1)} %param.7) | copy-start | bytes 1179652
  29.1 8.1 %copy-start.1 = (s32[12,16]{1,0:T(8,128)S(1)}, s32[12,16]{1,0:T(8,128)}, u32[]{:S(2)}) copy-start(s32[12,16]{1,0:T(8,128)} %param.10) | copy-start | bytes 2308
  29.1 15.4 %collective-permute-start.3 = (bf16[2,1024,128]{2,1,0:T(8,128)(2,1)S(1)}, bf16[2,1024,128]{2,1,0:T(8,128)(2,1)S(1)}, u32[]{:S(2)}, u32[]{:S(2)}) collective-permute-start(bf16[2,1024,128]{2,1,0:T(8,128)(2,1)S(1)} %get-tuple-element.184), channel_id=1, source_target_pairs={{0,4},{4,8},{8,12},{1,5},{5,9},{9,13},{2,6},{6,10},{10,14},{3,7},{... | collective-permute-start | bytes 1572872 | tf_op jit(solution)/shard_map/ppermute | solution.py:29
  30.5 14.1 %collective-permute-start.4 = (bf16[2,1024,128]{2,1,0:T(8,128)(2,1)S(1)}, bf16[2,1024,128]{2,1,0:T(8,128)(2,1)}, u32[]{:S(2)}, u32[]{:S(2)}) collective-permute-start(bf16[2,1024,128]{2,1,0:T(8,128)(2,1)S(1)} %get-tuple-element.185), channel_id=1, source_target_pairs={{4,0},{8,4},{12,8},{5,1},{9,5},{13,9},{6,2},{10,6},{14,10},{7,3},{... | collective-permute-start | bytes 1572872 | tf_op jit(solution)/shard_map/ppermute | solution.py:32
  32.2 5.7 %collective-permute-start = (bf16[384,128]{1,0:T(8,128)(2,1)S(1)}, bf16[384,128]{1,0:T(8,128)(2,1)S(1)}, u32[]{:S(2)}, u32[]{:S(2)}) collective-permute-start(bf16[384,128]{1,0:T(8,128)(2,1)S(1)} %bitcast.103), channel_id=1, source_target_pairs={{0,1},{1,0},{2,3},{3,2},{4,5},{5,4},{6,7},{7,6},{8,9},{9,8},{10,11... | collective-permute-start | bytes 294920 | tf_op jit(solution)/shard_map/ppermute | solution.py:106
  32.6 5.6 %collective-permute-start.1 = (bf16[384,128]{1,0:T(8,128)(2,1)S(1)}, bf16[384,128]{1,0:T(8,128)(2,1)S(1)}, u32[]{:S(2)}, u32[]{:S(2)}) collective-permute-start(bf16[384,128]{1,0:T(8,128)(2,1)S(1)} %bitcast.104), channel_id=1, source_target_pairs={{0,2},{1,3},{2,0},{3,1},{4,6},{5,7},{6,4},{7,5},{8,10},{9,11},{10,... | collective-permute-start | bytes 294920 | tf_op jit(solution)/shard_map/ppermute | solution.py:106
  34.6 7.6 %collective-permute-start.2 = (bf16[384,128]{1,0:T(8,128)(2,1)S(1)}, bf16[384,128]{1,0:T(8,128)(2,1)}, u32[]{:S(2)}, u32[]{:S(2)}) collective-permute-start(bf16[384,128]{1,0:T(8,128)(2,1)S(1)} %bitcast.105), channel_id=1, source_target_pairs={{0,3},{1,2},{2,1},{3,0},{4,7},{5,6},{6,5},{7,4},{8,11},{9,10},{10,... | collective-permute-start | bytes 294920 | tf_op jit(solution)/shard_map/ppermute | solution.py:106
